TPU v7x, 32 devices: a whole 2x2x4 slice. The times are simulated.
32 devices in a mesh: groups: 2 (over x), space: 8 (over z, y), dp: 2 (over core).
Axes of the slice: x: 2, y: 2, z: 4, core: 2. Of those that a mesh axis runs over, the one named last changes fastest.
Arguments:
- features: bfloat16 [4, 3072, 256], P(('groups', 'dp'), 'space'), parts along dimension 0, may hold values from -6 to 6
- positions: float32 [4, 3, 3072], P(('groups', 'dp'), None, 'space'), parts along dimension 0, may hold values from 0 to 3
- species: int32 [4, 3072], P(('groups', 'dp'), 'space'), parts along dimension 0, may hold values from 0 to 9
- ghost_ids: int32 [4, 8, 128], P(('groups', 'dp'), 'space'), parts along dimension 0, may hold values from -1 to 3071, as said below
- tile_mask: int32 [4, 8, 6, 8], P(('groups', 'dp'), 'space'), parts along dimension 0, may hold values from 0 to 1, as said below
- energy_grad: float32 [4, 3072], P(('groups', 'dp'), 'space'), parts along dimension 0, may hold values from -12 to 12
- w_proj: bfloat16 [256, 256], replicated, may hold values from -0.375 to 0.375
- w_radial: float32 [4, 256], replicated, may hold values from -3 to 3
- w_mix: float32 [4, 256], replicated, may hold values from -3 to 3
- w_update: bfloat16 [256, 256], replicated, may hold values from -0.375 to 0.375
- w_out: bfloat16 [256], replicated, may hold values from -0.375 to 0.375
- skip_gain: float32 [10, 256], replicated, may hold values from 0.1 to 1.9
Outputs:
- energies: float32 [4, 3072], P(('groups', 'dp'), 'space'), parts along dimension 0
- feature_grad: float32 [4, 3072, 256], P(('groups', 'dp'), 'space'), parts along dimension 0
- proj_grad: float32 [512, 256], P('groups'), parts along dimension 0
- radial_grad: float32 [8, 256], P('groups'), parts along dimension 0
- mix_grad: float32 [8, 256], P('groups'), parts along dimension 0
- update_grad: float32 [512, 256], P('groups'), parts along dimension 0
- out_grad: float32 [512], P('groups'), parts along dimension 0
- skip_grad: float32 [20, 256], P('groups'), parts along dimension 0
There are 2 independent parts, one for each index of `groups`. A program takes and returns all parts, laid end to end along the dimension named above; an argument that names none is the same for every part. Nothing has to cross between parts.
Inputs may be any that keep to these rules, and one draw needn't show every extreme that they name: `ghost_ids`: slot s of domain d holds -1 (an empty slot) or the index of an atom owned by domain d - 1 or d + 1. Live slots come before empty ones, and in every configuration some domain has all 128 slots live. `tile_mask`: 1 where the 64 owned atoms of a tile interact with the 64 near rows of another tile.
All inputs are finite; a program needn't handle non-finite values.
Results may differ from a plain program's by a relative error of at most 0.012.
The roundings to bfloat16 on the way count: a program that leaves them out, or rounds other values in their place, can miss the bound.
Values may be sent and summed in bfloat16 or wider, within the bound.
A program may use at most 64 MiB of HBM per device.

v0:
```python
import math

import jax
import jax.numpy as jnp
from jax import lax
from jax.sharding import PartitionSpec as P

neighbour_scale = 0.0625
radial_step = 0.8


def padded(array, sides, width):
    for axis, dim in sides:
        size, length = (lax.axis_size(axis), array.shape[dim])
        up = [(i, (i + 1) % size) for i in range(size - 1)]
        down = [(j, i) for i, j in up]
        last = lax.slice_in_dim(array, length - width, length, axis=dim)
        initial = lax.slice_in_dim(array, 0, width, axis=dim)
        before = lax.ppermute(last, axis, up)
        after = lax.ppermute(initial, axis, down)
        array = jnp.concatenate([before, array, after], axis=dim)
    return array


def edge_terms(own_pos, near_pos, pair_mask, radial_count):
    delta_x = near_pos[0][None, :] - own_pos[0][:, None]
    delta_y = near_pos[1][None, :] - own_pos[1][:, None]
    delta_z = near_pos[2][None, :] - own_pos[2][:, None]
    distance = jnp.sqrt(delta_x * delta_x + delta_y * delta_y + delta_z * delta_z)
    root_three = math.sqrt(3.0)
    shapes = jnp.stack(
        [
            jnp.ones_like(delta_x),
            delta_x,
            delta_y,
            delta_z,
            root_three * delta_x * delta_y,
            root_three * delta_y * delta_z,
            0.5 * (2.0 * delta_z * delta_z - delta_x * delta_x - delta_y * delta_y),
            root_three * delta_x * delta_z,
            0.5 * root_three * (delta_x * delta_x - delta_y * delta_y),
        ]
    )
    centres = radial_step * jnp.arange(radial_count).astype(jnp.float32)
    radial = jnp.exp(-jnp.square(distance[None] - centres[:, None, None]))
    weighted = shapes[:, None] * radial[None] * pair_mask[None, None]
    return weighted.reshape(9 * radial_count, delta_x.shape[0], delta_x.shape[1]).astype(
        jnp.bfloat16
    )


def pair_weights(tile_block, row_count, near_count):
    tile_size = row_count // tile_block.shape[0]
    spread = jnp.repeat(jnp.repeat(tile_block, tile_size, axis=0), tile_size, axis=1).astype(
        jnp.float32
    )
    apart = (
        jnp.arange(row_count, dtype=jnp.int32)[:, None]
        != jnp.arange(near_count, dtype=jnp.int32)[None, :]
    ).astype(jnp.float32)
    return spread * apart


def rows_pass(
    own_h,
    own_pos,
    pair_mask,
    species_ids,
    energy_cot,
    near_x,
    near_pos,
    w_radial,
    w_mix,
    w_update,
    w_out,
    skip_gain,
):
    radial_count, channels = w_radial.shape
    row_count = own_h.shape[0]
    precise = lax.Precision.HIGHEST
    edge_table = edge_terms(own_pos, near_pos, pair_mask, radial_count)
    moments = jnp.dot(
        edge_table.reshape(-1, near_x.shape[0]), near_x, preferred_element_type=jnp.float32
    )
    moments = moments.reshape(9, radial_count, row_count, channels) * neighbour_scale
    density = jnp.sum(w_radial[None, :, None, :] * moments, axis=1)
    invariants = jnp.stack(
        [
            density[0],
            density[0] * density[0],
            jnp.sum(density[1:4] * density[1:4], axis=0),
            jnp.sum(density[4:9] * density[4:9], axis=0),
        ]
    )
    mixed = jnp.sum(w_mix[:, None, :] * invariants, axis=0).astype(jnp.bfloat16)
    species_hot = (
        species_ids[:, None] == jnp.arange(skip_gain.shape[0], dtype=jnp.int32)[None, :]
    ).astype(jnp.float32)
    skip_row = jnp.dot(species_hot, skip_gain, precision=precise)
    own_float = own_h.astype(jnp.float32)
    update = jnp.dot(mixed, w_update, preferred_element_type=jnp.float32) + own_float * skip_row
    readout = w_out.astype(jnp.float32)
    active = jax.nn.silu(update)
    energy = jnp.sum(active * readout[None, :], axis=1)
    logistic = jax.nn.sigmoid(update)
    update_cot = (
        energy_cot[:, None] * readout[None, :] * (logistic * (1.0 + update * (1.0 - logistic)))
    )
    cot_bf = update_cot.astype(jnp.bfloat16)
    mixed_cot = lax.dot_general(
        cot_bf, w_update, (((1,), (1,)), ((), ())), preferred_element_type=jnp.float32
    )
    d_update = lax.dot_general(
        mixed, cot_bf, (((0,), (0,)), ((), ())), preferred_element_type=jnp.float32
    )
    d_mix = jnp.sum(mixed_cot[None] * invariants, axis=1)
    d_out = jnp.sum(energy_cot[:, None] * active, axis=0)
    d_skip = lax.dot_general(
        species_hot, update_cot * own_float, (((0,), (0,)), ((), ())), precision=precise
    )
    weighted = w_mix[:, None, :] * mixed_cot[None]
    leading = weighted[0] + 2.0 * weighted[1] * density[0]
    density_cot = jnp.concatenate(
        [
            leading[None],
            2.0 * weighted[2][None] * density[1:4],
            2.0 * weighted[3][None] * density[4:9],
        ],
        axis=0,
    )
    d_radial = jnp.sum(density_cot[:, None] * moments, axis=(0, 2))
    moment_cot = (density_cot[:, None] * w_radial[None, :, None, :]).astype(jnp.bfloat16)
    return (
        edge_table,
        moment_cot,
        energy,
        update_cot * skip_row,
        (d_update, d_mix, d_radial, d_out, d_skip),
    )


def body(
    features,
    positions,
    species,
    ghost_ids,
    tile_mask,
    energy_grad,
    w_proj,
    w_radial,
    w_mix,
    w_update,
    w_out,
    skip_gain,
):
    own_h = features[0]
    atom_count, channels = own_h.shape
    own_pos = positions[0]
    ghost_slots = ghost_ids[0, 0]
    ghosts = ghost_slots.shape[0]
    near_count = atom_count + ghosts
    domain = lax.axis_index("space")
    precise = lax.Precision.HIGHEST
    projected = jnp.dot(own_h, w_proj, preferred_element_type=jnp.float32).astype(jnp.bfloat16)
    own_spread = jnp.arange(atom_count, dtype=jnp.int32)
    lists = padded(ghost_slots, (("space", 0),), ghosts)
    spread = jnp.arange(3 * atom_count, dtype=jnp.int32)
    picker = (
        ((ghost_slots - (domain - 1) * atom_count)[:, None] == spread[None, :])
        & (ghost_slots >= 0)[:, None]
    ).astype(jnp.float32)
    wide_pos = padded(own_pos, (("space", 1),), atom_count)
    wide_rows = padded(projected, (("space", 0),), atom_count)
    ghost_pos = lax.dot_general(wide_pos, picker, (((1,), (1,)), ((), ())), precision=precise)
    ghost_rows = jnp.dot(
        picker.astype(jnp.bfloat16), wide_rows, preferred_element_type=jnp.float32
    ).astype(jnp.bfloat16)
    want_left = ((lists[:ghosts] - domain * atom_count)[:, None] == own_spread[None, :]).astype(
        jnp.float32
    )
    want_right = (
        (lists[2 * ghosts :] - domain * atom_count)[:, None] == own_spread[None, :]
    ).astype(jnp.float32)
    near_x = jnp.concatenate([projected, ghost_rows], axis=0)
    near_pos = jnp.concatenate([own_pos, ghost_pos], axis=1)
    mask = pair_weights(tile_mask[0, 0], atom_count, near_count)
    block_rows = math.gcd(atom_count, 32)
    block_count = atom_count // block_rows
    radial_count = w_radial.shape[0]
    pieces_all = (
        own_h.reshape(block_count, block_rows, channels),
        own_pos.reshape(3, block_count, block_rows).transpose(1, 0, 2),
        mask.reshape(block_count, block_rows, near_count),
        species[0].reshape(block_count, block_rows),
        energy_grad[0].reshape(block_count, block_rows),
    )

    def block_step(totals, pieces):
        edge_table, moment_cot, energy, skip_term, gradients = rows_pass(
            pieces[0],
            pieces[1],
            pieces[2],
            pieces[3],
            pieces[4],
            near_x,
            near_pos,
            w_radial,
            w_mix,
            w_update,
            w_out,
            skip_gain,
        )
        near_part = lax.dot_general(
            edge_table.reshape(-1, near_count),
            moment_cot.reshape(-1, channels),
            (((0,), (0,)), ((), ())),
            preferred_element_type=jnp.float32,
        )
        summed = tuple((total + extra for total, extra in zip(totals[:5], gradients)))
        return (summed + (totals[5] + near_part,), (energy, skip_term))

    initial = (
        jnp.zeros((channels, channels), jnp.float32),
        jnp.zeros((4, channels), jnp.float32),
        jnp.zeros((radial_count, channels), jnp.float32),
        jnp.zeros((channels,), jnp.float32),
        jnp.zeros(skip_gain.shape, jnp.float32),
        jnp.zeros((near_count, channels), jnp.float32),
    )
    totals, (energy, skip_term) = lax.scan(block_step, initial, pieces_all)
    d_update, d_mix, d_radial, d_out, d_skip, near_cot = totals
    near_cot = near_cot * neighbour_scale
    ghost_cot = near_cot[atom_count:]
    inbound = padded(ghost_cot, (("space", 0),), ghosts)
    returned = lax.dot_general(
        want_left, inbound[:ghosts], (((0,), (0,)), ((), ())), precision=precise
    ) + lax.dot_general(
        want_right, inbound[2 * ghosts :], (((0,), (0,)), ((), ())), precision=precise
    )
    proj_bf = (near_cot[:atom_count] + returned).astype(jnp.bfloat16)
    feature_grad = lax.dot_general(
        proj_bf, w_proj, (((1,), (1,)), ((), ())), preferred_element_type=jnp.float32
    )
    feature_grad = feature_grad + skip_term.reshape(atom_count, channels)
    proj_part = lax.dot_general(
        own_h, proj_bf, (((0,), (0,)), ((), ())), preferred_element_type=jnp.float32
    )
    proj_total, update_total, mix_total, radial_total, out_total, skip_total = lax.psum(
        (proj_part, d_update, d_mix, d_radial, d_out, d_skip), ("space", "dp")
    )
    grad_scale = (
        lax.axis_size("space") * lax.axis_size("dp") * atom_count * features.shape[0]
    ) ** (-0.5)
    return (
        energy.reshape(1, atom_count),
        feature_grad.reshape(1, atom_count, channels),
        proj_total * grad_scale,
        radial_total * grad_scale,
        mix_total * grad_scale,
        update_total * grad_scale,
        out_total * grad_scale,
        skip_total * grad_scale,
    )


def solution(mesh):
    in_specs = (
        P(("groups", "dp"), "space", None),
        P(("groups", "dp"), None, "space"),
        P(("groups", "dp"), "space"),
        P(("groups", "dp"), "space", None),
        P(("groups", "dp"), "space", None, None),
        P(("groups", "dp"), "space"),
        P(),
        P(),
        P(),
        P(),
        P(),
        P(),
    )
    out_specs = (
        P(("groups", "dp"), "space"),
        P(("groups", "dp"), "space", None),
        P("groups", None),
        P("groups", None),
        P("groups", None),
        P("groups", None),
        P("groups"),
        P("groups", None),
    )
    return jax.shard_map(body, mesh=mesh, in_specs=in_specs, out_specs=out_specs, check_vma=False)
```

profile of v0, /device:TPU:0, one launch (start us, length us, event | category | flops | bytes accessed | tf_op | source)
XLA Modules:
  0.0 261.5 jit_solution(15860516694577191131)
XLA Ops:
  7.2 0.7 copy.39
  7.9 1.3 collective-permute-start.1
  9.2 5.5 %collective-permute-start = (f32[3,384]{1,0:T(4,128)S(1)}, f32[3,384]{1,0:T(4,128)S(1)}, u32[]{:S(2)}, u32[]{:S(2)}) collective-permute-start(f32[3,384]{1,0:T(4,128)S(1)} %bitcast.159), channel_id=1, source_target_pairs={{0,2},{2,4},{4,6},{6,8},{8,10},{10,12},{12,14},{1,3},{3,5},{5,7},{... | collective-permute-start | bytes 13832 | tf_op jit(solution)/shard_map/ppermute | solution.py:19
  14.8 1.1 convolution_convert_fusion
  15.9 1.3 collective-permute-start.3
  17.2 6.1 %collective-permute-start.2 = (bf16[384,256]{1,0:T(8,128)(2,1)S(1)}, bf16[384,256]{1,0:T(8,128)(2,1)}, u32[]{:S(2)}, u32[]{:S(2)}) collective-permute-start(bf16[384,256]{1,0:T(8,128)(2,1)S(1)} %convolution_convert_fusion), channel_id=1, source_target_pairs={{0,2},{2,4},{4,6},{6,8},{8,10},{10,12},{12,14},{1,3},{3,5},{5,7},{... | collective-permute-start | bytes 589832 | tf_op jit(solution)/shard_map/ppermute | solution.py:19
  23.3 1.3 collective-permute-start.6
  26.0 0.7 fusion.61
  29.1 4.8 %collective-permute-start.4 = (s32[128]{0:T(128)S(1)}, s32[128]{0:T(128)S(1)}, u32[]{:S(2)}, u32[]{:S(2)}) collective-permute-start(s32[128]{0:T(128)S(1)} %bitcast.164), channel_id=1, source_target_pairs={{0,2},{2,4},{4,6},{6,8},{8,10},{10,12},{12,14},{1,3},{3,5},{5,7},{... | collective-permute-start | bytes 1544 | tf_op jit(solution)/shard_map/ppermute | solution.py:19
  34.0 1.3 collective-permute-done.4
  35.8 1.4 convolution_convert_fusion.1
  37.4 57.7 %while.25 = (s32[]{:T(128)}, f32[256,256]{1,0:T(8,128)S(1)}, f32[4,256]{1,0:T(4,128)S(1)}, f32[4,256]{1,0:T(4,128)S(1)}, f32[256]{0:T(256)S(1)}, /*index=5*/f32[...) while((s32[]{:T(128)}, f32[256,256]{1,0:T(8,128)S(1)}, ...), condition=%wide.region_9.10_spmd.clone, body=%wide.region_0.9_spmd.clone.sunk | while | flops 626230400 | bytes 19709776 | solution.py:230
  51.0 0.7 convolution_add_fusion.11
  89.5 0.7 convolution_add_fusion.11
  95.2 1.3 collective-permute-start.7
  96.5 4.9 %collective-permute-start.5 = (f32[128,256]{1,0:T(8,128)S(1)}, f32[128,256]{1,0:T(8,128)S(1)}, u32[]{:S(2)}, u32[]{:S(2)}) collective-permute-start(f32[128,256]{1,0:T(8,128)S(1)} %slice.78), channel_id=1, source_target_pairs={{0,2},{2,4},{4,6},{6,8},{8,10},{10,12},{12,14},{1,3},{3,5},{5,7},{... | collective-permute-start | bytes 393224 | tf_op jit(solution)/shard_map/ppermute | solution.py:19
  102.0 0.8 copy.26
  102.8 58.6 %all-reduce = (f32[4,256]{1,0:T(4,128)S(1)}, f32[4,256]{1,0:T(4,128)S(1)}, f32[256]{0:T(256)S(1)}, f32[10,256]{1,0:T(8,128)S(1)}) all-reduce(f32[4,256]{1,0:T(4,128)S(1)} %get-tuple-element.125, f32[4,256]{1,0:T(4,128)S(1)} %get-tuple-element.126, ...), channel_id=1, replica_groups=mesh['groups'=2,'space'=8,'dp'=2] {'space','dp'}, use_global_device_ids=true, to_apply=%region_11.12 | all-reduce | flops 4864 | bytes 38912 | tf_op jit(solution)/shard_map/psum | solution.py:248
  163.6 1.0 convolution_bitcast_fusion
  165.1 1.0 fusion.35
  166.1 85.8 %all-reduce.4.cloned.1.call-done = (f32[256,256]{0,1:T(8,128)}, f32[256,256]{0,1:T(8,128)}) async-done(((f32[256,256]{0,1:T(8,128)}, f32[256,256]{0,1:T(8,128)}), (f32[256,256]{0,1:T(8,128)}, f32[256,256]{0,1:T(8,128)})) %all-reduce.4.cloned.1.call-update) | async-done | bytes 524304 | tf_op jit(solution)/shard_map/psum | solution.py:248
  251.9 1.1 broadcast_multiply_fusion.6
  253.0 0.8 copy.27
  253.8 0.8 copy.28
  (581 shorter events, 61.2 us)
Async XLA Ops:
  7.2 7.6 %copy-start = (bf16[256,256]{1,0:T(8,128)(2,1)S(1)}, bf16[256,256]{1,0:T(8,128)(2,1)}, u32[]{:S(2)}) copy-start(bf16[256,256]{1,0:T(8,128)(2,1)} %param.20) | copy-start | bytes 393220
  7.2 244.7 %all-reduce.4.cloned.1.call-start = ((), (), s32[]{:S(2)}) async-start(), calls=%async_computation | async-start | bytes 1048576 | tf_op jit(solution)/shard_map/psum | solution.py:248
  7.9 27.3 %collective-permute-start.1 = (f32[3,384]{1,0:T(4,128)S(1)}, f32[3,384]{1,0:T(4,128)S(1)}, u32[]{:S(2)}, u32[]{:S(2)}) collective-permute-start(f32[3,384]{1,0:T(4,128)S(1)} %bitcast.158), channel_id=1, source_target_pairs={{2,0},{4,2},{6,4},{8,6},{10,8},{12,10},{14,12},{3,1},{5,3},{7,5},{... | collective-permute-start | bytes 13832 | tf_op jit(solution)/shard_map/ppermute | solution.py:20
  9.2 26.0 %collective-permute-start = (f32[3,384]{1,0:T(4,128)S(1)}, f32[3,384]{1,0:T(4,128)S(1)}, u32[]{:S(2)}, u32[]{:S(2)}) collective-permute-start(f32[3,384]{1,0:T(4,128)S(1)} %bitcast.159), channel_id=1, source_target_pairs={{0,2},{2,4},{4,6},{6,8},{8,10},{10,12},{12,14},{1,3},{3,5},{5,7},{... | collective-permute-start | bytes 13832 | tf_op jit(solution)/shard_map/ppermute | solution.py:19
  15.9 19.9 %collective-permute-start.3 = (bf16[384,256]{1,0:T(8,128)(2,1)S(1)}, bf16[384,256]{1,0:T(8,128)(2,1)}, u32[]{:S(2)}, u32[]{:S(2)}) collective-permute-start(bf16[384,256]{1,0:T(8,128)(2,1)S(1)} %convolution_convert_fusion), channel_id=1, source_target_pairs={{2,0},{4,2},{6,4},{8,6},{10,8},{12,10},{14,12},{3,1},{5,3},{7,5},{... | collective-permute-start | bytes 589832 | tf_op jit(solution)/shard_map/ppermute | solution.py:20
  17.2 18.6 %collective-permute-start.2 = (bf16[384,256]{1,0:T(8,128)(2,1)S(1)}, bf16[384,256]{1,0:T(8,128)(2,1)}, u32[]{:S(2)}, u32[]{:S(2)}) collective-permute-start(bf16[384,256]{1,0:T(8,128)(2,1)S(1)} %convolution_convert_fusion), channel_id=1, source_target_pairs={{0,2},{2,4},{4,6},{6,8},{8,10},{10,12},{12,14},{1,3},{3,5},{5,7},{... | collective-permute-start | bytes 589832 | tf_op jit(solution)/shard_map/ppermute | solution.py:19
  23.3 5.8 %collective-permute-start.6 = (s32[128]{0:T(128)}, s32[128]{0:T(128)S(1)}, u32[]{:S(2)}, u32[]{:S(2)}) collective-permute-start(s32[128]{0:T(128)} %bitcast.163), channel_id=1, source_target_pairs={{2,0},{4,2},{6,4},{8,6},{10,8},{12,10},{14,12},{3,1},{5,3},{7,5},{... | collective-permute-start | bytes 1544 | tf_op jit(solution)/shard_map/ppermute | solution.py:20
  27.6 0.7 copy-start.5
  27.6 0.8 copy-start.6
  27.6 0.9 copy-start.7
  27.6 1.5 copy-start.10
  29.1 6.1 %collective-permute-start.4 = (s32[128]{0:T(128)S(1)}, s32[128]{0:T(128)S(1)}, u32[]{:S(2)}, u32[]{:S(2)}) collective-permute-start(s32[128]{0:T(128)S(1)} %bitcast.164), channel_id=1, source_target_pairs={{0,2},{2,4},{4,6},{6,8},{8,10},{10,12},{12,14},{1,3},{3,5},{5,7},{... | collective-permute-start | bytes 1544 | tf_op jit(solution)/shard_map/ppermute | solution.py:19
  35.7 1.6 copy-start.1
  35.8 1.6 copy-start.2
  35.8 1.6 copy-start.3
  35.8 1.6 copy-start.4
  35.8 1.6 copy-start.8
  35.8 1.6 copy-start.9
  35.8 1.6 copy-start.11
  95.2 67.5 %collective-permute-start.7 = (f32[128,256]{1,0:T(8,128)S(1)}, f32[128,256]{1,0:T(8,128)S(1)}, u32[]{:S(2)}, u32[]{:S(2)}) collective-permute-start(f32[128,256]{1,0:T(8,128)S(1)} %slice.78), channel_id=1, source_target_pairs={{2,0},{4,2},{6,4},{8,6},{10,8},{12,10},{14,12},{3,1},{5,3},{7,5},{... | collective-permute-start | bytes 393224 | tf_op jit(solution)/shard_map/ppermute | solution.py:20
  96.5 66.7 %collective-permute-start.5 = (f32[128,256]{1,0:T(8,128)S(1)}, f32[128,256]{1,0:T(8,128)S(1)}, u32[]{:S(2)}, u32[]{:S(2)}) collective-permute-start(f32[128,256]{1,0:T(8,128)S(1)} %slice.78), channel_id=1, source_target_pairs={{0,2},{2,4},{4,6},{6,8},{8,10},{10,12},{12,14},{1,3},{3,5},{5,7},{... | collective-permute-start | bytes 393224 | tf_op jit(solution)/shard_map/ppermute | solution.py:19
Sparse Core Ops, SparseCore 0:
  164.7 87.1 all-reduce.3
where the time goes:
time: 262 us; the launch traced here: 261 us
  waiting for transfers between devices  87.6 us (33%)
  blocking collectives  58.6 us (22%)
  matrix products  34.3 us (13%)
  other arithmetic  30.3 us (12%)
  starting transfers between devices  26.5 us (10%)
  between operations  14.4 us (5%)
  local copies, waits for them, and re-layouts  6.86 us (3%)
  loops' own time  2.83 us (1%)
    psum x1, waiting for transfers between devices, body(): lax.psum((proj_part, d_update, d_mix, d_radial, d_out, d_skip), ('space',...  85.8 us
    psum x1, blocking collectives, body(): lax.psum((proj_part, d_update, d_mix, d_radial, d_out, d_skip), ('space',...  58.6 us
    ppermute x4, starting transfers between devices, padded(): before = lax.ppermute(last, axis, up)  21.3 us
    dot_general x12, matrix products, block_step(): lax.dot_general(edge_table.reshape(-1, near_count), moment_cot.reshape(-1...  7.96 us
    while x84, other arithmetic  6.53 us
    dot_general x12, matrix products, rows_pass(): jnp.dot(edge_table.reshape(-1, near_x.shape[0]), near_x, preferred_elemen...  6.3 us
  transfers between devices with their start and end apart: 9, of which 3 were waited for; matrix products, arithmetic and copies ran while one was open for 4% of the time, Pallas kernels for 0%

commit v1 on v0

v1 whole, which is shorter than its diff:
```python
import functools
import math

import jax
import jax.numpy as jnp
from jax import lax
from jax.experimental import pallas as pl
from jax.experimental.pallas import tpu as pltpu
from jax.sharding import PartitionSpec as P

neighbour_scale = 0.0625
radial_step = 0.8
MESH = pl.DeviceIdType.MESH
HIGH = lax.Precision.HIGHEST
F32 = jnp.float32
BF16 = jnp.bfloat16


def loop(count, step):
    if count <= 16:
        for i in range(count):
            step(i)
    else:
        lax.fori_loop(0, count, lambda i, c: (step(i), c)[1], 0)


def edge_products(dx, dy, dz, weight, radial_count):
    xx, yy, zz = dx * dx, dy * dy, dz * dz
    r = jnp.sqrt(xx + yy + zz)
    radial = []
    for k in range(radial_count):
        t = r - radial_step * k if k else r
        radial.append(jnp.exp(-(t * t)) * weight)
    r3 = math.sqrt(3.0)
    shapes = [
        None,
        dx,
        dy,
        dz,
        r3 * dx * dy,
        r3 * dy * dz,
        0.5 * (2.0 * zz - xx - yy),
        r3 * dx * dz,
        0.5 * r3 * (xx - yy),
    ]
    return [b if y is None else y * b for y in shapes for b in radial]


def nt_dot(a, b, precision=None):
    return lax.dot_general(
        a, b, (((1,), (1,)), ((), ())), preferred_element_type=F32, precision=precision
    )


def tn_dot(a, b):
    return lax.dot_general(a, b, (((0,), (0,)), ((), ())), preferred_element_type=F32)


class Reduce:
    def __init__(self, refs, chunks, rows, stride, lin, total, parts):
        self.send, self.recv, self.back, self.s1, self.r1, self.s2, self.r2 = refs
        self.chunks, self.rows, self.stride = chunks, rows, stride
        self.lin, self.total, self.parts = lin, total, parts
        self.mine = lax.div(lin, stride)
        self.everyone = stride == 1 and chunks == total

    def peer(self, index):
        return {"space": lax.div(index, self.parts), "dp": lax.rem(index, self.parts)}

    def block(self, ref, chunk):
        return ref.at[pl.ds(pl.multiple_of(chunk * self.rows, self.rows), self.rows)]

    def owned(self, step):
        if self.everyone:
            step()
        else:
            pl.when((lax.rem(self.lin, self.stride) == 0) & (self.mine < self.chunks))(step)

    def unless_self(self, chunk, step):
        pl.when(chunk * self.stride != self.lin)(step)

    def out_copy(self, chunk):
        return pltpu.make_async_remote_copy(
            src_ref=self.block(self.send, chunk),
            dst_ref=self.recv.at[self.lin],
            send_sem=self.s1.at[chunk],
            recv_sem=self.r1.at[self.lin],
            device_id=self.peer(chunk * self.stride),
            device_id_type=MESH,
        )

    def in_copy(self, sender):
        return pltpu.make_async_remote_copy(
            src_ref=self.recv.at[sender],
            dst_ref=self.recv.at[sender],
            send_sem=self.s1.at[0],
            recv_sem=self.r1.at[sender],
            device_id=self.peer(sender),
            device_id_type=MESH,
        )

    def back_copy(self, target):
        return pltpu.make_async_remote_copy(
            src_ref=self.block(self.back, self.mine),
            dst_ref=self.block(self.back, self.mine),
            send_sem=self.s2.at[target],
            recv_sem=self.r2.at[self.mine],
            device_id=self.peer(target),
            device_id_type=MESH,
        )

    def home_copy(self, chunk):
        return pltpu.make_async_remote_copy(
            src_ref=self.block(self.back, chunk),
            dst_ref=self.block(self.back, chunk),
            send_sem=self.s2.at[0],
            recv_sem=self.r2.at[chunk],
            device_id=self.peer(chunk * self.stride),
            device_id_type=MESH,
        )

    def each_chunk(self, act):
        if self.everyone:
            loop(self.chunks - 1, lambda o: act(lax.rem(self.lin + 1 + o, self.chunks)))
        else:
            loop(self.chunks, lambda q: self.unless_self(q, lambda: act(q)))

    def each_peer(self, act):
        loop(self.total - 1, lambda o: act(lax.rem(self.lin + 1 + o, self.total)))

    def scatter(self):
        self.each_chunk(lambda q: self.out_copy(q).start())

    def collect(self, scale):
        def step():
            self.recv[self.lin] = self.block(self.send, self.mine)[...]
            self.each_peer(lambda t: self.in_copy(t).wait_recv())
            if self.total <= 16:
                acc = self.recv[0].astype(F32)
                for i in range(1, self.total):
                    acc = acc + self.recv[i].astype(F32)
            else:
                acc = lax.fori_loop(
                    1,
                    self.total,
                    lambda i, a: a + self.recv[i].astype(F32),
                    self.recv[0].astype(F32),
                )
            self.block(self.back, self.mine)[...] = (acc * scale).astype(self.back.dtype)
            self.each_peer(lambda t: self.back_copy(t).start())

        self.owned(step)

    def finish(self):
        self.each_chunk(lambda q: self.home_copy(q).wait_recv())

    def drain(self):
        self.each_chunk(lambda q: self.out_copy(q).wait_send())
        self.owned(lambda: self.each_peer(lambda t: self.back_copy(t).wait_send()))


def kernel(dims, *refs):
    spaces, parts, n, ghosts, channels, radial_count, species_count, tiles, scale = dims
    (
        feat_ref,
        pos_ref,
        spec_ref,
        ghost_ref,
        tile_ref,
        eg_ref,
        wproj_ref,
        wrad_ref,
        wmix_ref,
        wupd_ref,
        wout_ref,
        skip_ref,
        energy_ref,
        fgrad_ref,
        pgrad_ref,
        rgrad_ref,
        mgrad_ref,
        ugrad_ref,
        ograd_ref,
        sgrad_ref,
        table,
        turned,
        moments,
        density,
        near_x,
        small,
        near_pos,
        columns,
        near_columns,
        tile_pad,
        mask_rows,
        mask_cols,
        gain_pad,
        skip_row,
        mixed,
        cot_b,
        work,
        mcot,
        part_energy,
        turned_h,
        near_cot,
        nbr_x,
        nbr_small,
        ghost_in,
        u_send,
        u_recv,
        u_back,
        p_send,
        p_recv,
        p_back,
        s_send,
        s_recv,
        s_back,
        x_sem,
        u_s1,
        u_r1,
        u_s2,
        u_r2,
        p_s1,
        p_r1,
        p_s2,
        p_r2,
        s_s1,
        s_r1,
        s_s2,
        s_r2,
    ) = refs
    m = n + ghosts
    pk = 9 * radial_count
    total = spaces * parts
    me = lax.axis_index("space")
    lin = me * parts + lax.axis_index("dp")
    matrix_chunks = channels // 16
    matrix_stride = max(1, total // matrix_chunks)
    upd = Reduce(
        (u_send, u_recv, u_back, u_s1, u_r1, u_s2, u_r2),
        matrix_chunks, 16, matrix_stride, lin, total, parts,
    )
    prj = Reduce(
        (p_send, p_recv, p_back, p_s1, p_r1, p_s2, p_r2),
        matrix_chunks, 16, matrix_stride, lin, total, parts,
    )
    sml = Reduce(
        (s_send, s_recv, s_back, s_s1, s_r1, s_s2, s_r2), 3, 8, total // 4, lin, total, parts
    )

    @pl.when(me == 0)
    def _():
        nbr_x[0] = jnp.zeros((n, channels), BF16)
        nbr_small[0] = jnp.zeros((8, m), F32)
        ghost_in[0] = jnp.zeros((ghosts, channels), F32)

    @pl.when(me == spaces - 1)
    def _():
        nbr_x[1] = jnp.zeros((n, channels), BF16)
        nbr_small[1] = jnp.zeros((8, m), F32)
        ghost_in[1] = jnp.zeros((ghosts, channels), F32)

    barrier = pltpu.get_barrier_semaphore()
    upd.each_peer(
        lambda t: pl.semaphore_signal(
            barrier, inc=1, device_id=upd.peer(t), device_id_type=MESH
        )
    )

    small[...] = jnp.zeros((8, m), F32)
    small[0:3, 0:n] = pos_ref[0]
    small[3:4, 0:ghosts] = ghost_ref[0].astype(F32)
    small[4:5, 0:n] = eg_ref[...]
    small[5:6, 0:n] = spec_ref[...].astype(F32)
    own_h = feat_ref[0]
    near_x[0:n] = jnp.dot(own_h, wproj_ref[...], preferred_element_type=F32).astype(BF16)
    pl.semaphore_wait(barrier, total - 1)

    dp_at = lax.axis_index("dp")

    def exchange(ref, into, lane):
        pairs = []
        for side, target, there in ((0, me + 1, me < spaces - 1), (1, me - 1, me > 0)):
            source_there = me > 0 if side == 0 else me < spaces - 1
            copy = pltpu.make_async_remote_copy(
                src_ref=ref,
                dst_ref=into.at[side],
                send_sem=x_sem.at[lane, side],
                recv_sem=x_sem.at[lane + 1, side],
                device_id={"space": target, "dp": dp_at},
                device_id_type=MESH,
            )
            pairs.append((copy, there, source_there))
        return pairs

    def start(pairs):
        for copy, there, _ in pairs:
            pl.when(there)(copy.start)

    def arrive(pairs):
        for copy, _, source_there in pairs:
            pl.when(source_there)(copy.wait_recv)

    def sent(pairs):
        for copy, there, _ in pairs:
            pl.when(there)(copy.wait_send)

    rows_out = exchange(near_x.at[0:n], nbr_x, 0)
    small_out = exchange(small, nbr_small, 2)
    start(small_out)
    start(rows_out)

    tile_pad[...] = jnp.zeros(tile_pad.shape, F32)
    tile_pad[0 : tiles[0], 0 : tiles[1]] = tile_ref[0, 0].astype(F32)
    tile_size = n // tiles[0]
    flags = tile_pad[...]
    flags_turned = flags.T[0:8, :]
    at_m = lax.div(lax.broadcasted_iota(jnp.int32, (8, m), 1), tile_size)
    at_n = lax.div(lax.broadcasted_iota(jnp.int32, (8, n), 1), tile_size)
    by_row = jnp.zeros((8, m), F32)
    by_col = jnp.zeros((8, n), F32)
    for u in range(tiles[1]):
        by_row = jnp.where(at_m == u, flags[:, u : u + 1], by_row)
    for t in range(tiles[0]):
        by_col = jnp.where(at_n == t, flags_turned[:, t : t + 1], by_col)
    for t in range(8):
        mask_rows[t] = jnp.broadcast_to(by_row[t : t + 1], (8, m))
        mask_cols[t] = jnp.broadcast_to(by_col[t : t + 1], (8, n))
    columns[...] = small[...].T
    near_pos[...] = small[...]

    lanes = 128

    def fill_rows(block, chunks):
        at = pl.multiple_of(block * 16, 16)
        cols = columns[pl.ds(at, 16), :]
        ox, oy, oz = cols[:, 0:1], cols[:, 1:2], cols[:, 2:3]
        tile = lax.div(at, tile_size)
        for chunk in chunks:
            where = slice(chunk * lanes, (chunk + 1) * lanes)
            weight = jnp.broadcast_to(mask_rows[tile, 0:1, where], (16, lanes))
            if chunk * lanes < n:
                row = lax.broadcasted_iota(jnp.int32, (16, lanes), 0) + at
                col = lax.broadcasted_iota(jnp.int32, (16, lanes), 1) + chunk * lanes
                weight = jnp.where(row == col, 0.0, weight)
            dx = near_pos[0:1, where] - ox
            dy = near_pos[1:2, where] - oy
            dz = near_pos[2:3, where] - oz
            for i, v in enumerate(edge_products(dx, dy, dz, weight, radial_count)):
                table[i, pl.ds(at, 16), where] = v.astype(BF16)

    def fill_turned(block, own):
        at = pl.multiple_of(block * 16, 16)
        cols = columns[pl.ds(at, 16), :] if own else near_columns[pl.ds(at - n, 16), :]
        nx, ny, nz = cols[:, 0:1], cols[:, 1:2], cols[:, 2:3]
        tile = lax.div(at, tile_size)
        for chunk in range(n // lanes):
            where = slice(chunk * lanes, (chunk + 1) * lanes)
            weight = jnp.broadcast_to(mask_cols[tile, 0:1, where], (16, lanes))
            if own:
                row = lax.broadcasted_iota(jnp.int32, (16, lanes), 0) + at
                col = lax.broadcasted_iota(jnp.int32, (16, lanes), 1) + chunk * lanes
                weight = jnp.where(row == col, 0.0, weight)
            dx = nx - small[0:1, where]
            dy = ny - small[1:2, where]
            dz = nz - small[2:3, where]
            for i, v in enumerate(edge_products(dx, dy, dz, weight, radial_count)):
                to = slice(i * n + chunk * lanes, i * n + (chunk + 1) * lanes)
                turned[pl.ds(at, 16), to] = v.astype(BF16)

    own_chunks = range(n // lanes)
    far_chunks = range(n // lanes, m // lanes)

    @pl.loop(0, n // 16)
    def _(block):
        fill_rows(block, own_chunks)

    @pl.loop(0, n // 16)
    def _(block):
        fill_turned(block, True)

    turned_h[...] = own_h.T
    gain_pad[...] = jnp.zeros(gain_pad.shape, F32)
    gain_pad[0:species_count] = skip_ref[...]
    hot = (
        columns[0:n, 5:6] == lax.broadcasted_iota(jnp.int32, (n, 16), 1).astype(F32)
    ).astype(F32)
    skip_row[...] = jnp.dot(hot, gain_pad[...], precision=HIGH, preferred_element_type=F32)

    arrive(small_out)
    arrive(rows_out)
    base = (me * n).astype(F32)
    id_col = columns[0:ghosts, 3:4]
    id_row = small[3:4, 0:ghosts]
    live_col = jnp.where(id_col < 0.0, -1e6, id_col - base)
    live_row = jnp.where(id_row < 0.0, -1e6, id_row - base)
    at_lane = lax.broadcasted_iota(jnp.int32, (ghosts, n), 1).astype(F32)
    at_row = lax.broadcasted_iota(jnp.int32, (n, ghosts), 0).astype(F32)
    far_rows = jnp.zeros((ghosts, channels), F32)
    far_pos = jnp.zeros((8, ghosts), F32)
    for side, shift in ((0, float(n)), (1, -float(n))):
        pick = (live_col + shift == at_lane).astype(F32).astype(BF16)
        far_rows += jnp.dot(pick, nbr_x[side], preferred_element_type=F32)
        pick_row = (live_row + shift == at_row).astype(F32)
        far_pos += jnp.dot(
            nbr_small[side, :, 0:n], pick_row, precision=HIGH, preferred_element_type=F32
        )
    near_x[n:m] = far_rows.astype(BF16)
    near_pos[:, n:m] = far_pos
    near_columns[...] = far_pos.T

    @pl.loop(0, n // 16)
    def _(block):
        fill_rows(block, far_chunks)

    @pl.loop(0, 9)
    def _(p):
        at = p * radial_count
        lhs = table[pl.ds(at, radial_count)].reshape(radial_count * n, m)
        out = jnp.dot(lhs, near_x[...], preferred_element_type=F32) * neighbour_scale
        moments[pl.ds(at, radial_count)] = out.reshape(radial_count, n, channels)

    def halves():
        return [slice(h * lanes, (h + 1) * lanes) for h in range(channels // lanes)]

    def invariants_of(dens):
        return [
            dens[0],
            dens[0] * dens[0],
            dens[1] * dens[1] + dens[2] * dens[2] + dens[3] * dens[3],
            dens[4] * dens[4]
            + dens[5] * dens[5]
            + dens[6] * dens[6]
            + dens[7] * dens[7]
            + dens[8] * dens[8],
        ]

    @pl.loop(0, n // 16)
    def _(block):
        rows = pl.ds(pl.multiple_of(block * 16, 16), 16)
        for where in halves():
            weights = [wrad_ref[k : k + 1, where] for k in range(radial_count)]
            dens = []
            for p in range(9):
                acc = weights[0] * moments[p * radial_count, rows, where]
                for k in range(1, radial_count):
                    acc += weights[k] * moments[p * radial_count + k, rows, where]
                density[p, rows, where] = acc
                dens.append(acc)
            inv = invariants_of(dens)
            acc = wmix_ref[0:1, where] * inv[0]
            for q in range(1, 4):
                acc += wmix_ref[q : q + 1, where] * inv[q]
            mixed[rows, where] = acc.astype(BF16)

    work[...] = jnp.dot(mixed[...], wupd_ref[...], preferred_element_type=F32)

    def node_step(block, totals):
        rows = pl.ds(pl.multiple_of(block * 16, 16), 16)
        grad = columns[rows, 4:5]
        sums, energy = [], None
        for h, where in enumerate(halves()):
            own = feat_ref[0, rows, where].astype(F32)
            skip = skip_row[rows, where]
            update = work[rows, where] + own * skip
            readout = wout_ref[0:1, where].astype(F32)
            logistic = jax.nn.sigmoid(update)
            active = update * logistic
            share = active * readout
            energy = share if energy is None else energy + share
            cot = grad * readout * (logistic * (1.0 + update * (1.0 - logistic)))
            cot_b[rows, where] = cot.astype(BF16)
            fgrad_ref[0, rows, where] = cot * skip
            work[rows, where] = cot * own
            sums.append(totals[h] + grad * active)
        part_energy[rows, :] = energy
        return tuple(sums)

    zero = jnp.zeros((16, lanes), F32)
    out_sums = lax.fori_loop(
        0, n // 16, node_step, tuple(zero for _ in range(channels // lanes))
    )
    mcot[...] = nt_dot(cot_b[...], wupd_ref[...])
    u_send[...] = tn_dot(mixed[...], cot_b[...]).astype(BF16)
    upd.scatter()

    def grad_step(block, totals):
        rows = pl.ds(pl.multiple_of(block * 16, 16), 16)
        rad, mix = list(totals[0]), list(totals[1])
        for h, where in enumerate(halves()):
            dens = [density[p, rows, where] for p in range(9)]
            cot = mcot[rows, where]
            inv = invariants_of(dens)
            weighted = []
            for q in range(4):
                at = h * 4 + q
                mix[at] = mix[at] + cot * inv[q]
                weighted.append(wmix_ref[q : q + 1, where] * cot)
            w2, w3 = 2.0 * weighted[2], 2.0 * weighted[3]
            weights = [wrad_ref[k : k + 1, where] for k in range(radial_count)]
            for p in range(9):
                if p == 0:
                    dcot = weighted[0] + 2.0 * weighted[1] * dens[0]
                else:
                    dcot = (w2 if p < 4 else w3) * dens[p]
                for k in range(radial_count):
                    i = p * radial_count + k
                    at = h * radial_count + k
                    rad[at] = rad[at] + dcot * moments[i, rows, where]
                    table[i, rows, where] = (dcot * weights[k]).astype(BF16)
        return tuple(rad), tuple(mix)

    count = channels // lanes
    rad_sums, mix_sums = lax.fori_loop(
        0,
        n // 16,
        grad_step,
        (tuple(zero for _ in range(radial_count * count)), tuple(zero for _ in range(4 * count))),
    )

    hot_turned = (
        small[5:6, 0:n] == lax.broadcasted_iota(jnp.int32, (16, n), 0).astype(F32)
    ).astype(F32)
    s_send[...] = jnp.zeros(s_send.shape, F32)
    for h, where in enumerate(halves()):
        for k in range(radial_count):
            s_send[k : k + 1, where] = jnp.sum(
                rad_sums[h * radial_count + k], axis=0, keepdims=True
            )
        for q in range(4):
            s_send[4 + q : 5 + q, where] = jnp.sum(mix_sums[h * 4 + q], axis=0, keepdims=True)
        s_send[18:19, where] = jnp.sum(out_sums[h], axis=0, keepdims=True)
    s_send[8 : 8 + species_count] = jnp.dot(
        hot_turned, work[...], precision=HIGH, preferred_element_type=F32
    )[0:species_count]
    sml.scatter()

    @pl.loop(0, (m - n) // 16)
    def _(block):
        fill_turned(block + n // 16, False)

    step_pk = 6 if pk % 6 == 0 else 1

    def back_part(first, rows):
        near_cot[first : first + rows] = jnp.zeros((rows, channels), F32)

        @pl.loop(0, pk // step_pk)
        def _(j):
            lhs = turned[
                first : first + rows,
                pl.ds(pl.multiple_of(j * (step_pk * n), lanes), step_pk * n),
            ]
            rhs = table[pl.ds(j * step_pk, step_pk), :, 0:channels].reshape(
                step_pk * n, channels
            )
            near_cot[first : first + rows] += jnp.dot(lhs, rhs, preferred_element_type=F32)

        near_cot[first : first + rows] = near_cot[first : first + rows] * neighbour_scale

    back_part(n, ghosts)
    ghost_out = exchange(near_cot.at[n:m], ghost_in, 4)
    start(ghost_out)
    upd.collect(scale)
    back_part(0, n)
    sml.collect(scale)
    energy_ref[...] = jnp.sum(part_energy[...].T, axis=0, keepdims=True)

    arrive(ghost_out)
    returned = near_cot[0:n]
    for side in range(2):
        ids = nbr_small[side, 3:4, 0:ghosts] - base
        want = (ids == at_row).astype(F32)
        returned += jnp.dot(want, ghost_in[side], precision=HIGH, preferred_element_type=F32)
    proj_b = returned.astype(BF16)
    p_send[...] = jnp.dot(turned_h[...], proj_b, preferred_element_type=F32).astype(BF16)
    prj.scatter()
    fgrad_ref[0] = fgrad_ref[0] + nt_dot(proj_b, wproj_ref[...])
    prj.collect(scale)

    upd.finish()
    ugrad_ref[...] = u_back[...].astype(F32)
    sml.finish()
    rgrad_ref[...] = s_back[0:radial_count]
    mgrad_ref[...] = s_back[4:8]
    sgrad_ref[...] = s_back[8 : 8 + species_count]
    ograd_ref[...] = s_back[18:19]
    prj.finish()
    pgrad_ref[...] = p_back[...].astype(F32)

    sent(small_out)
    sent(rows_out)
    sent(ghost_out)
    upd.drain()
    sml.drain()
    prj.drain()


def body(spaces, parts, *args):
    features, positions, species, ghost_ids, tile_mask = args[:5]
    wout_at = 10
    args = list(args)
    args[wout_at] = args[wout_at].reshape(1, -1)
    _, n, channels = features.shape
    ghosts = ghost_ids.shape[-1]
    radial_count = args[7].shape[0]
    species_count = args[11].shape[0]
    tiles = tile_mask.shape[2:]
    m = n + ghosts
    pk = 9 * radial_count
    total = spaces * parts
    scale = (spaces * parts * n * features.shape[0]) ** (-0.5)
    chunks = channels // 16
    vmem = pltpu.VMEM
    dma = pltpu.SemaphoreType.DMA
    dims = (spaces, parts, n, ghosts, channels, radial_count, species_count, tiles, scale)
    scratch = [
        vmem((pk, n, m), BF16),
        vmem((m, pk * n), BF16),
        vmem((pk, n, channels), F32),
        vmem((9, n, channels), F32),
        vmem((m, channels), BF16),
        vmem((8, m), F32),
        vmem((8, m), F32),
        vmem((m, 8), F32),
        vmem((ghosts, 8), F32),
        vmem((8, 128), F32),
        vmem((8, 8, m), F32),
        vmem((8, 8, n), F32),
        vmem((16, channels), F32),
        vmem((n, channels), F32),
        vmem((n, channels), BF16),
        vmem((n, channels), BF16),
        vmem((n, channels), F32),
        vmem((n, channels), F32),
        vmem((n, 128), F32),
        vmem((channels, n), BF16),
        vmem((m, channels), F32),
        vmem((2, n, channels), BF16),
        vmem((2, 8, m), F32),
        vmem((2, ghosts, channels), F32),
    ]
    for _ in range(2):
        scratch += [
            vmem((channels, channels), BF16),
            vmem((total, 16, channels), BF16),
            vmem((channels, channels), BF16),
        ]
    scratch += [vmem((24, channels), F32), vmem((total, 8, channels), F32), vmem((24, channels), F32)]
    scratch += [dma((6, 2))]
    for _ in range(2):
        scratch += [dma((chunks,)), dma((total,)), dma((total,)), dma((chunks,))]
    scratch += [dma((3,)), dma((total,)), dma((total,)), dma((3,))]
    whole = pl.BlockSpec(memory_space=pltpu.VMEM)
    shapes = [
        (1, n),
        (1, n, channels),
        (channels, channels),
        (radial_count, channels),
        (4, channels),
        (channels, channels),
        (1, channels),
        (species_count, channels),
    ]
    outs = pl.pallas_call(
        functools.partial(kernel, dims),
        out_shape=[jax.ShapeDtypeStruct(s, F32) for s in shapes],
        in_specs=[whole] * len(args),
        out_specs=[whole] * len(shapes),
        scratch_shapes=scratch,
        compiler_params=pltpu.CompilerParams(
            collective_id=0, has_side_effects=True, vmem_limit_bytes=60 * 1024 * 1024
        ),
    )(*args)
    outs = list(outs)
    outs[6] = outs[6].reshape(channels)
    return tuple(outs)


def solution(mesh):
    in_specs = (
        P(("groups", "dp"), "space", None),
        P(("groups", "dp"), None, "space"),
        P(("groups", "dp"), "space"),
        P(("groups", "dp"), "space", None),
        P(("groups", "dp"), "space", None, None),
        P(("groups", "dp"), "space"),
        P(),
        P(),
        P(),
        P(),
        P(),
        P(),
    )
    out_specs = (
        P(("groups", "dp"), "space"),
        P(("groups", "dp"), "space", None),
        P("groups", None),
        P("groups", None),
        P("groups", None),
        P("groups", None),
        P("groups"),
        P("groups", None),
    )
    step = functools.partial(body, mesh.shape["space"], mesh.shape["dp"])
    return jax.shard_map(step, mesh=mesh, in_specs=in_specs, out_specs=out_specs, check_vma=False)
```

time: 262 us -> 70.1 us (0.27)
  waiting for transfers between devices: 87.6 us -> 0 us
  Pallas kernels: 0 us -> 59.1 us
  blocking collectives: 58.6 us -> 0 us
  matrix products: 34.3 us -> 0 us
  other arithmetic: 30.3 us -> 0 us
  starting transfers between devices: 26.5 us -> 0 us
  between operations: 14.4 us -> 0.67 us
  local copies, waits for them, and re-layouts: 6.86 us -> 10 us
  loops' own time: 2.83 us -> 0 us
    psum x1 -> x0, waiting for transfers between devices: 85.8 us -> none  [body(): lax.psum((proj_part, d_update, d_mix, d_radial, d_out, d_skip), ('space',...]
    pallas_call x0 -> x1, Pallas kernels: none -> 59.1 us  [body(): pl.pallas_call(functools.partial(kernel, dims), out_shape=[jax.ShapeDtype...]
    psum x1 -> x0, blocking collectives: 58.6 us -> none  [body(): lax.psum((proj_part, d_update, d_mix, d_radial, d_out, d_skip), ('space',...]
    dot_general x91 -> x0, matrix products: 34.3 us -> none  [the longest x12 7.96 us: block_step(): lax.dot_general(edge_table.reshape(-1, near_count), moment_cot.reshape(-1...]
    ppermute x8 -> x0, starting transfers between devices: 26.5 us -> none  [the longest x4 21.3 us: padded(): before = lax.ppermute(last, axis, up)]
    mul x78 -> x0, other arithmetic: 8.07 us -> none  [the longest x12 4.02 us: edge_terms(): weighted = shapes[:, None] * radial[None] * pair_mask[None, None]]
    convert_element_type x37 -> x0, other arithmetic: 6.55 us -> none  [the longest x12 4.19 us: edge_terms(): weighted.reshape(9 * radial_count, delta_x.shape[0], delta_x.shape[1])]
    while x84 -> x0, other arithmetic: 6.53 us -> none
  transfers between devices with their start and end apart: 9 -> 0, of which waited for: 3 -> 0; matrix products, arithmetic and copies ran while one was open for 4% -> 0% of each run, Pallas kernels for 0% -> 0%
where the time goes in v1:
time: 70.1 us; the launch traced here: 69.8 us
  Pallas kernels  59.1 us (84%)
  local copies, waits for them, and re-layouts  10 us (14%)
    pallas_call x1, Pallas kernels, body(): pl.pallas_call(functools.partial(kernel, dims), out_shape=[jax.ShapeDtype...  59.1 us
    unnamed x26, local copies, waits for them, and re-layouts  8.78 us

profile of v1, /device:TPU:0, one launch (start us, length us, event | category | flops | bytes accessed | tf_op | source)
XLA Modules:
  0.0 69.8 jit_solution(13636804874367785585)
XLA Ops:
  0.6 0.0 copy-start.3
  0.6 1.2 %reshape.22.refs_10_ = bf16[1,256]{1,0:T(2,128)(2,1)} reshape(bf16[256]{0:T(256)(128)(2,1)} %param.22) | data formatting | bytes 1024 | tf_op jit(solution)/shard_map/reshape | solution.py:602
  1.9 1.3 %copy.21.refs_4_ = s32[1,1,6,8]{3,2,1,0:T(8,128)} copy(s32[1,1,6,8]{3,1,2,0:T(1,128)} %param.16) | data formatting | bytes 384 | tf_op args[4]
  3.1 0.0 copy-done.3
  3.1 0.6 copy.20.refs_1_
  3.7 59.1 %shard_map.179 = (f32[1,384]{1,0:T(1,128)}, f32[1,384,256]{2,1,0:T(8,128)}, f32[256,256]{1,0:T(8,128)}, f32[4,256]{1,0:T(4,128)}, f32[4,256]{1,0:T(4,128)}, /*in...) custom-call(bf16[1,384,256]{2,1,0:T(8,128)(2,1)} %refs_0_.1, f32[1,3,384]{2,1,0:T(4,128)} %copy.20.refs_1_, ...), custom_call_target="tpu_custom_call" | custom-call | tf_op jit(solution)/shard_map/pallas_call | solution.py:664
  62.9 0.0 copy-start.6
  62.9 0.7 copy-done.6
  63.6 0.6 copy.30
  64.1 0.0 copy-start.1
  64.1 1.8 %copy.31 = f32[1,384,256]{2,1,0:T(8,128)} copy(f32[1,384,256]{2,1,0:T(8,128)} %get-tuple-element.33) | data formatting | bytes 786432
  65.9 0.0 copy-done.1
  65.9 0.0 copy-start.5
  65.9 0.7 %copy.32 = f32[256,256]{1,0:T(8,128)} copy(f32[256,256]{1,0:T(8,128)S(1)} %copy-done.1) | data formatting | bytes 524288
  66.6 0.0 copy-done.5
  66.7 0.6 copy.33
  67.2 0.1 copy-done.4
  67.3 0.6 copy.34
  67.9 0.0 copy-done
  67.9 0.7 %copy.35 = f32[256,256]{1,0:T(8,128)} copy(f32[256,256]{1,0:T(8,128)S(1)} %copy-done) | data formatting | bytes 524288
  68.6 0.0 copy-done.7
  68.6 0.6 copy.36
  69.2 0.0 copy-done.2
  69.2 0.6 copy.37
  (4 shorter events, 0.0 us)
Async XLA Ops:
  0.6 2.5 %copy-start.3 = (f32[1,3,384]{2,0,1:T(1,128)S(1)}, f32[1,3,384]{2,0,1:T(1,128)}, u32[]{:S(2)}) copy-start(f32[1,3,384]{2,0,1:T(1,128)} %param.13) | copy-start | bytes 13828
  62.9 0.7 copy-start.6
  64.1 1.8 %copy-start.1 = (f32[256,256]{1,0:T(8,128)S(1)}, f32[256,256]{1,0:T(8,128)}, u32[]{:S(2)}) copy-start(f32[256,256]{1,0:T(8,128)} %get-tuple-element.34) | copy-start | bytes 786436
  65.9 0.7 %copy-start.5 = (f32[4,256]{1,0:T(4,128)S(1)}, f32[4,256]{1,0:T(4,128)}, u32[]{:S(2)}) copy-start(f32[4,256]{1,0:T(4,128)} %get-tuple-element.35) | copy-start | bytes 12292
  65.9 2.0 %copy-start = (f32[256,256]{1,0:T(8,128)S(1)}, f32[256,256]{1,0:T(8,128)}, u32[]{:S(2)}) copy-start(f32[256,256]{1,0:T(8,128)} %get-tuple-element.37) | copy-start | bytes 786436
  66.7 0.7 copy-start.4
  67.9 0.7 %copy-start.7 = (f32[1,256]{1,0:T(1,128)S(1)}, f32[1,256]{1,0:T(1,128)}, u32[]{:S(2)}) copy-start(f32[1,256]{1,0:T(1,128)} %get-tuple-element.22) | copy-start | bytes 3076
  67.9 1.3 %copy-start.2 = (f32[10,256]{1,0:T(8,128)S(1)}, f32[10,256]{1,0:T(8,128)}, u32[]{:S(2)}) copy-start(f32[10,256]{1,0:T(8,128)} %get-tuple-element.39) | copy-start | bytes 30724

commit v2 on v1

--- a/solution.py
+++ b/solution.py
@@ -204,6 +204,9 @@
         turned_h,
         near_cot,
         nbr_x,
+        sent_x,
+        sent_cot,
+        wout_row,
         nbr_small,
         ghost_in,
         u_send,
@@ -250,15 +253,15 @@
 
     @pl.when(me == 0)
     def _():
-        nbr_x[0] = jnp.zeros((n, channels), BF16)
+        nbr_x[0] = jnp.zeros((ghosts, channels), BF16)
         nbr_small[0] = jnp.zeros((8, m), F32)
-        ghost_in[0] = jnp.zeros((ghosts, channels), F32)
+        ghost_in[0] = jnp.zeros((ghosts, channels), BF16)
 
     @pl.when(me == spaces - 1)
     def _():
-        nbr_x[1] = jnp.zeros((n, channels), BF16)
+        nbr_x[1] = jnp.zeros((ghosts, channels), BF16)
         nbr_small[1] = jnp.zeros((8, m), F32)
-        ghost_in[1] = jnp.zeros((ghosts, channels), F32)
+        ghost_in[1] = jnp.zeros((ghosts, channels), BF16)
 
     barrier = pltpu.get_barrier_semaphore()
     upd.each_peer(
@@ -267,8 +270,10 @@
         )
     )
 
+    wout_row[...] = jnp.broadcast_to(wout_ref[...].astype(F32)[None, :], (8, channels))
     small[...] = jnp.zeros((8, m), F32)
-    small[0:3, 0:n] = pos_ref[0]
+    for axis in range(3):
+        small[axis : axis + 1, 0:n] = pos_ref[axis]
     small[3:4, 0:ghosts] = ghost_ref[0].astype(F32)
     small[4:5, 0:n] = eg_ref[...]
     small[5:6, 0:n] = spec_ref[...].astype(F32)
@@ -278,9 +283,10 @@
 
     dp_at = lax.axis_index("dp")
 
-    def exchange(ref, into, lane):
+    def exchange(sources, into, lane):
         pairs = []
         for side, target, there in ((0, me + 1, me < spaces - 1), (1, me - 1, me > 0)):
+            ref = sources[1 - side]
             source_there = me > 0 if side == 0 else me < spaces - 1
             copy = pltpu.make_async_remote_copy(
                 src_ref=ref,
@@ -305,13 +311,12 @@
         for copy, there, _ in pairs:
             pl.when(there)(copy.wait_send)
 
-    rows_out = exchange(near_x.at[0:n], nbr_x, 0)
-    small_out = exchange(small, nbr_small, 2)
+    small_out = exchange((small, small), nbr_small, 2)
     start(small_out)
-    start(rows_out)
 
     tile_pad[...] = jnp.zeros(tile_pad.shape, F32)
-    tile_pad[0 : tiles[0], 0 : tiles[1]] = tile_ref[0, 0].astype(F32)
+    for t in range(tiles[0]):
+        tile_pad[t : t + 1, 0 : tiles[1]] = tile_ref[t].astype(F32)
     tile_size = n // tiles[0]
     flags = tile_pad[...]
     flags_turned = flags.T[0:8, :]
@@ -375,6 +380,18 @@
     def _(block):
         fill_rows(block, own_chunks)
 
+    arrive(small_out)
+    base = (me * n).astype(F32)
+    at_lane = lax.broadcasted_iota(jnp.int32, (ghosts, n), 1).astype(F32)
+    at_row = lax.broadcasted_iota(jnp.int32, (n, ghosts), 0).astype(F32)
+    for side in range(2):
+        asked = nbr_small[side, :, 0:ghosts].T[:, 3:4] - base
+        pick = (asked == at_lane).astype(F32).astype(BF16)
+        picked = jnp.dot(pick, near_x[0:n], preferred_element_type=F32)
+        sent_x[side] = picked.astype(BF16)
+    rows_out = exchange((sent_x.at[0], sent_x.at[1]), nbr_x, 0)
+    start(rows_out)
+
     @pl.loop(0, n // 16)
     def _(block):
         fill_turned(block, True)
@@ -387,27 +404,27 @@
     ).astype(F32)
     skip_row[...] = jnp.dot(hot, gain_pad[...], precision=HIGH, preferred_element_type=F32)
 
-    arrive(small_out)
-    arrive(rows_out)
-    base = (me * n).astype(F32)
-    id_col = columns[0:ghosts, 3:4]
     id_row = small[3:4, 0:ghosts]
-    live_col = jnp.where(id_col < 0.0, -1e6, id_col - base)
     live_row = jnp.where(id_row < 0.0, -1e6, id_row - base)
-    at_lane = lax.broadcasted_iota(jnp.int32, (ghosts, n), 1).astype(F32)
-    at_row = lax.broadcasted_iota(jnp.int32, (n, ghosts), 0).astype(F32)
-    far_rows = jnp.zeros((ghosts, channels), F32)
-    far_pos = jnp.zeros((8, ghosts), F32)
+    terms, picks = [], []
     for side, shift in ((0, float(n)), (1, -float(n))):
-        pick = (live_col + shift == at_lane).astype(F32).astype(BF16)
-        far_rows += jnp.dot(pick, nbr_x[side], preferred_element_type=F32)
-        pick_row = (live_row + shift == at_row).astype(F32)
-        far_pos += jnp.dot(
-            nbr_small[side, :, 0:n], pick_row, precision=HIGH, preferred_element_type=F32
-        )
-    near_x[n:m] = far_rows.astype(BF16)
+        rest = nbr_small[side, :, 0:n]
+        high = rest.astype(BF16).astype(F32)
+        rest = rest - high
+        middle = rest.astype(BF16).astype(F32)
+        low = rest - middle
+        terms.append(jnp.concatenate([high, middle, low, jnp.zeros_like(low)], axis=0))
+        picks.append((live_row + shift == at_row).astype(F32).astype(BF16))
+    split = jnp.dot(
+        jnp.concatenate(terms, axis=1).astype(BF16),
+        jnp.concatenate(picks, axis=0),
+        preferred_element_type=F32,
+    )
+    far_pos = (split[0:8] + split[8:16]) + split[16:24]
     near_pos[:, n:m] = far_pos
     near_columns[...] = far_pos.T
+    arrive(rows_out)
+    near_x[n:m] = (nbr_x[0].astype(F32) + nbr_x[1].astype(F32)).astype(BF16)
 
     @pl.loop(0, n // 16)
     def _(block):
@@ -417,7 +434,7 @@
     def _(p):
         at = p * radial_count
         lhs = table[pl.ds(at, radial_count)].reshape(radial_count * n, m)
-        out = jnp.dot(lhs, near_x[...], preferred_element_type=F32) * neighbour_scale
+        out = jnp.dot(lhs, near_x[...], preferred_element_type=F32)
         moments[pl.ds(at, radial_count)] = out.reshape(radial_count, n, channels)
 
     def halves():
@@ -439,7 +456,9 @@
     def _(block):
         rows = pl.ds(pl.multiple_of(block * 16, 16), 16)
         for where in halves():
-            weights = [wrad_ref[k : k + 1, where] for k in range(radial_count)]
+            weights = [
+                wrad_ref[k : k + 1, where] * neighbour_scale for k in range(radial_count)
+            ]
             dens = []
             for p in range(9):
                 acc = weights[0] * moments[p * radial_count, rows, where]
@@ -455,15 +474,17 @@
 
     work[...] = jnp.dot(mixed[...], wupd_ref[...], preferred_element_type=F32)
 
+    node_rows = math.gcd(n, 64)
+
     def node_step(block, totals):
-        rows = pl.ds(pl.multiple_of(block * 16, 16), 16)
+        rows = pl.ds(pl.multiple_of(block * node_rows, node_rows), node_rows)
         grad = columns[rows, 4:5]
         sums, energy = [], None
         for h, where in enumerate(halves()):
             own = feat_ref[0, rows, where].astype(F32)
             skip = skip_row[rows, where]
             update = work[rows, where] + own * skip
-            readout = wout_ref[0:1, where].astype(F32)
+            readout = wout_row[0:1, where]
             logistic = jax.nn.sigmoid(update)
             active = update * logistic
             share = active * readout
@@ -476,9 +497,9 @@
         part_energy[rows, :] = energy
         return tuple(sums)
 
-    zero = jnp.zeros((16, lanes), F32)
+    zero = jnp.zeros((node_rows, lanes), F32)
     out_sums = lax.fori_loop(
-        0, n // 16, node_step, tuple(zero for _ in range(channels // lanes))
+        0, n // node_rows, node_step, tuple(zero for _ in range(channels // lanes))
     )
     mcot[...] = nt_dot(cot_b[...], wupd_ref[...])
     u_send[...] = tn_dot(mixed[...], cot_b[...]).astype(BF16)
@@ -511,6 +532,7 @@
         return tuple(rad), tuple(mix)
 
     count = channels // lanes
+    zero = jnp.zeros((16, lanes), F32)
     rad_sums, mix_sums = lax.fori_loop(
         0,
         n // 16,
@@ -524,7 +546,7 @@
     s_send[...] = jnp.zeros(s_send.shape, F32)
     for h, where in enumerate(halves()):
         for k in range(radial_count):
-            s_send[k : k + 1, where] = jnp.sum(
+            s_send[k : k + 1, where] = neighbour_scale * jnp.sum(
                 rad_sums[h * radial_count + k], axis=0, keepdims=True
             )
         for q in range(4):
@@ -555,10 +577,10 @@
             )
             near_cot[first : first + rows] += jnp.dot(lhs, rhs, preferred_element_type=F32)
 
-        near_cot[first : first + rows] = near_cot[first : first + rows] * neighbour_scale
 
     back_part(n, ghosts)
-    ghost_out = exchange(near_cot.at[n:m], ghost_in, 4)
+    sent_cot[...] = (near_cot[n:m] * neighbour_scale).astype(BF16)
+    ghost_out = exchange((sent_cot, sent_cot), ghost_in, 4)
     start(ghost_out)
     upd.collect(scale)
     back_part(0, n)
@@ -566,11 +588,15 @@
     energy_ref[...] = jnp.sum(part_energy[...].T, axis=0, keepdims=True)
 
     arrive(ghost_out)
-    returned = near_cot[0:n]
-    for side in range(2):
-        ids = nbr_small[side, 3:4, 0:ghosts] - base
-        want = (ids == at_row).astype(F32)
-        returned += jnp.dot(want, ghost_in[side], precision=HIGH, preferred_element_type=F32)
+    wants = [
+        (nbr_small[side, 3:4, 0:ghosts] - base == at_row).astype(F32).astype(BF16)
+        for side in range(2)
+    ]
+    returned = near_cot[0:n] * neighbour_scale + jnp.dot(
+        jnp.concatenate(wants, axis=1),
+        ghost_in[...].reshape(2 * ghosts, channels),
+        preferred_element_type=F32,
+    )
     proj_b = returned.astype(BF16)
     p_send[...] = jnp.dot(turned_h[...], proj_b, preferred_element_type=F32).astype(BF16)
     prj.scatter()
@@ -595,12 +621,24 @@
     prj.drain()
 
 
+def hand_over(*refs):
+    count = len(refs) // 2
+    sems = refs[-1]
+    copies = [
+        pltpu.make_async_copy(refs[i], refs[count + i], sems.at[i]) for i in range(count)
+    ]
+    for copy in copies:
+        copy.start()
+    for copy in copies:
+        copy.wait()
+
+
 def body(spaces, parts, *args):
     features, positions, species, ghost_ids, tile_mask = args[:5]
-    wout_at = 10
     args = list(args)
-    args[wout_at] = args[wout_at].reshape(1, -1)
     _, n, channels = features.shape
+    args[1] = positions.reshape(3, 1, n)
+    args[4] = tile_mask.reshape(tile_mask.shape[2], 1, tile_mask.shape[3])
     ghosts = ghost_ids.shape[-1]
     radial_count = args[7].shape[0]
     species_count = args[11].shape[0]
@@ -635,9 +673,12 @@
         vmem((n, 128), F32),
         vmem((channels, n), BF16),
         vmem((m, channels), F32),
-        vmem((2, n, channels), BF16),
+        vmem((2, ghosts, channels), BF16),
+        vmem((2, ghosts, channels), BF16),
+        vmem((ghosts, channels), BF16),
+        vmem((8, channels), F32),
         vmem((2, 8, m), F32),
-        vmem((2, ghosts, channels), F32),
+        vmem((2, ghosts, channels), BF16),
     ]
     for _ in range(2):
         scratch += [
@@ -671,6 +712,13 @@
             collective_id=0, has_side_effects=True, vmem_limit_bytes=60 * 1024 * 1024
         ),
     )(*args)
+    outs = pl.pallas_call(
+        hand_over,
+        out_shape=[jax.ShapeDtypeStruct(s, F32) for s in shapes],
+        in_specs=[pl.BlockSpec(memory_space=pl.ANY)] * len(shapes),
+        out_specs=[pl.BlockSpec(memory_space=pl.ANY)] * len(shapes),
+        scratch_shapes=[dma((len(shapes),))],
+    )(*outs)
     outs = list(outs)
     outs[6] = outs[6].reshape(channels)
     return tuple(outs)

time: 70.1 us -> 84.5 us (1.21)
  Pallas kernels: 59.1 us -> 83.7 us
  local copies, waits for them, and re-layouts: 10 us -> 0 us
    pallas_call x0 -> x1, Pallas kernels: none -> 29.8 us  [body(): pl.pallas_call(hand_over, out_shape=[jax.ShapeDtypeStruct(s, F32) for s i...]
    unnamed x26 -> x0, local copies, waits for them, and re-layouts: 8.78 us -> none
    pallas_call x1, Pallas kernels: 59.1 us -> 53.9 us  [body(): pl.pallas_call(functools.partial(kernel, dims), out_shape=[jax.ShapeDtype...]
    reshape x1 -> x0, local copies, waits for them, and re-layouts: 1.23 us -> none  [body(): args[wout_at] = args[wout_at].reshape(1, -1)]
where the time goes in v2:
time: 84.5 us; the launch traced here: 84.3 us
  Pallas kernels  83.7 us (99%)
    pallas_call x1, Pallas kernels, body(): pl.pallas_call(functools.partial(kernel, dims), out_shape=[jax.ShapeDtype...  53.9 us
    pallas_call x1, Pallas kernels, body(): pl.pallas_call(hand_over, out_shape=[jax.ShapeDtypeStruct(s, F32) for s i...  29.8 us

profile of v2, /device:TPU:0, one launch (start us, length us, event | category | flops | bytes accessed | tf_op | source)
XLA Modules:
  0.0 84.3 jit_solution(15738016763656536553)
XLA Ops:
  0.6 53.9 %shard_map.179 = (f32[1,384]{1,0:T(1,128)}, f32[1,384,256]{2,1,0:T(8,128)}, f32[256,256]{1,0:T(8,128)}, f32[4,256]{1,0:T(4,128)}, f32[4,256]{1,0:T(4,128)}, /*in...) custom-call(bf16[1,384,256]{2,1,0:T(8,128)(2,1)} %refs_0_.1, f32[3,1,384]{2,1,0:T(1,128)} %bitcast.3, ...), custom_call_target="tpu_custom_call" | custom-call | tf_op jit(solution)/shard_map/pallas_call | solution.py:705
  54.5 29.8 %shard_map.180 = (f32[1,384]{1,0:T(1,128)}, f32[1,384,256]{2,1,0:T(8,128)}, f32[256,256]{1,0:T(8,128)}, f32[4,256]{1,0:T(4,128)}, f32[4,256]{1,0:T(4,128)}, /*in...) custom-call(f32[1,384]{1,0:T(1,128)} %get-tuple-element.24.refs_0_, ...), custom_call_target="tpu_custom_call" | custom-call | tf_op jit(solution)/shard_map/pallas_call | solution.py:715

commit v3 on v2

--- a/solution.py
+++ b/solution.py
@@ -623,14 +623,8 @@
 
 def hand_over(*refs):
     count = len(refs) // 2
-    sems = refs[-1]
-    copies = [
-        pltpu.make_async_copy(refs[i], refs[count + i], sems.at[i]) for i in range(count)
-    ]
-    for copy in copies:
-        copy.start()
-    for copy in copies:
-        copy.wait()
+    for source, target in zip(refs[:count], refs[count:]):
+        target[...] = source[...]
 
 
 def body(spaces, parts, *args):
@@ -715,9 +709,8 @@
     outs = pl.pallas_call(
         hand_over,
         out_shape=[jax.ShapeDtypeStruct(s, F32) for s in shapes],
-        in_specs=[pl.BlockSpec(memory_space=pl.ANY)] * len(shapes),
-        out_specs=[pl.BlockSpec(memory_space=pl.ANY)] * len(shapes),
-        scratch_shapes=[dma((len(shapes),))],
+        in_specs=[whole] * len(shapes),
+        out_specs=[whole] * len(shapes),
     )(*outs)
     outs = list(outs)
     outs[6] = outs[6].reshape(channels)

time: 84.5 us -> 56.8 us (0.67)
  Pallas kernels: 83.7 us -> 56 us
    pallas_call x1, Pallas kernels: 29.8 us -> 2.12 us  [body(): pl.pallas_call(hand_over, out_shape=[jax.ShapeDtypeStruct(s, F32) for s i...]
where the time goes in v3:
time: 56.8 us; the launch traced here: 56.6 us
  Pallas kernels  56 us (99%)
  between operations  0.65 us (1%)
    pallas_call x1, Pallas kernels, body(): pl.pallas_call(functools.partial(kernel, dims), out_shape=[jax.ShapeDtype...  53.9 us
    pallas_call x1, Pallas kernels, body(): pl.pallas_call(hand_over, out_shape=[jax.ShapeDtypeStruct(s, F32) for s i...  2.12 us

profile of v3, /device:TPU:0, one launch (start us, length us, event | category | flops | bytes accessed | tf_op | source)
XLA Modules:
  0.0 56.6 jit_solution(4147338062599218970)
XLA Ops:
  0.6 53.9 %shard_map.179 = (f32[1,384]{1,0:T(1,128)}, f32[1,384,256]{2,1,0:T(8,128)}, f32[256,256]{1,0:T(8,128)}, f32[4,256]{1,0:T(4,128)}, f32[4,256]{1,0:T(4,128)}, /*in...) custom-call(bf16[1,384,256]{2,1,0:T(8,128)(2,1)} %refs_0_.1, f32[3,1,384]{2,1,0:T(1,128)} %bitcast.3, ...), custom_call_target="tpu_custom_call" | custom-call | tf_op jit(solution)/shard_map/pallas_call | solution.py:699
  54.5 2.1 %shard_map.180 = (f32[1,384]{1,0:T(1,128)}, f32[1,384,256]{2,1,0:T(8,128)}, f32[256,256]{1,0:T(8,128)}, f32[4,256]{1,0:T(4,128)}, f32[4,256]{1,0:T(4,128)}, /*in...) custom-call(f32[1,384]{1,0:T(1,128)} %get-tuple-element.24.refs_0_, ...), custom_call_target="tpu_custom_call" | custom-call | tf_op jit(solution)/shard_map/pallas_call | solution.py:709
